TPU v7x, 32 devices: a whole 2x2x4 slice. The times are simulated.
32 devices in a mesh: grp: 2 (over y), row: 4 (over x, core), col: 4 (over z).
Axes of the slice: x: 2, y: 2, z: 4, core: 2. Of those that a mesh axis runs over, the one named last changes fastest.
Arguments:
- amplitudes: bfloat16 [32768, 16384], P(('grp', 'row'), 'col'), parts along dimension 0, may hold values from -0.046875 to 0.046875
- cholesky: bfloat16 [1024, 32768], P('row', ('grp', 'col')), parts along dimension 1, may hold values from -1.078125 to 1.078125
- occ_index: int32 [32768], P('grp'), parts along dimension 0, may hold values from 0 to 31
- vir_index: int32 [32768], P('grp'), parts along dimension 0, may hold values from 0 to 511
- eps_occ: float32 [64], P('grp'), parts along dimension 0, may hold values from -2 to -0.3
- eps_vir: float32 [1024], P('grp'), parts along dimension 0, may hold values from 0.2 to 3
Outputs:
- new_amplitudes: bfloat16 [32768, 16384], P(('grp', 'row'), 'col'), parts along dimension 0
There are 2 independent parts, one for each index of `grp`. A program takes and returns all parts, laid end to end along the dimension named above; each array names one. Nothing has to cross between parts.
All inputs are finite; a program needn't handle non-finite values.
Results may differ from a plain program's by a relative error of at most 0.0056.
Values may be sent and summed in bfloat16 or wider, within the bound.
No kernel may reach another device: no remote copies, remote signals or barrier semaphores. Data moves between devices by JAX's collectives and lax.ppermute only.
A program may use at most 128 MiB of HBM per device.

v0:
```python
import jax
import jax.numpy as jnp
from jax import lax
from jax.sharding import PartitionSpec as P


def pair_gaps(occ_index, vir_index, eps_occ, eps_vir, begin_pair, pair_count):
    occ_rows = lax.dynamic_slice_in_dim(occ_index, begin_pair, pair_count, 0)
    vir_rows = lax.dynamic_slice_in_dim(vir_index, begin_pair, pair_count, 0)
    occ_table = jnp.arange(eps_occ.shape[0], dtype=jnp.int32)
    vir_table = jnp.arange(eps_vir.shape[0], dtype=jnp.int32)
    occ_energy = jnp.sum(
        jnp.where(occ_rows[:, None] == occ_table[None, :], eps_occ[None, :], 0.0), axis=1
    )
    vir_energy = jnp.sum(
        jnp.where(vir_rows[:, None] == vir_table[None, :], eps_vir[None, :], 0.0), axis=1
    )
    return vir_energy - occ_energy


def local(amplitudes, cholesky, occ_index, vir_index, eps_occ, eps_vir):
    row_position = lax.axis_index("row")
    col_position = lax.axis_index("col")
    rows_block, cols_block = amplitudes.shape
    all_pairs = lax.all_gather(cholesky, "col", axis=1, tiled=True)
    chol_rows = lax.all_to_all(all_pairs, "row", split_axis=1, concat_axis=0, tiled=True)
    dressed = lax.psum_scatter(
        jnp.dot(chol_rows, amplitudes, preferred_element_type=jnp.float32),
        "row",
        scatter_dimension=0,
        tiled=True,
    )
    ydress = (cholesky.astype(jnp.float32) + dressed).astype(jnp.bfloat16)
    contract = (((0,), (0,)), ((), ()))
    ydress_pairs = lax.all_gather(ydress, "col", axis=1, tiled=True)
    ydress_rows = lax.all_to_all(ydress_pairs, "row", split_axis=1, concat_axis=0, tiled=True)
    gram = lax.dot_general(
        ydress_rows,
        lax.all_gather(ydress, "row", axis=0, tiled=True),
        contract,
        preferred_element_type=jnp.float32,
    )
    gap_rows = pair_gaps(
        occ_index, vir_index, eps_occ, eps_vir, row_position * rows_block, rows_block
    )
    gap_cols = pair_gaps(
        occ_index, vir_index, eps_occ, eps_vir, col_position * cols_block, cols_block
    )
    return (-gram / (gap_rows[:, None] + gap_cols[None, :])).astype(jnp.bfloat16)


def solution(mesh):
    return jax.shard_map(
        local,
        mesh=mesh,
        in_specs=(
            P(("grp", "row"), "col"),
            P("row", ("grp", "col")),
            P("grp"),
            P("grp"),
            P("grp"),
            P("grp"),
        ),
        out_specs=P(("grp", "row"), "col"),
        check_vma=False,
    )
```

profile of v0, /device:TPU:6, one launch (start us, length us, event | category | flops | bytes accessed | tf_op | source)
XLA Modules:
  0.0 793.6 jit_solution(10187947766805902085)
XLA Ops:
  6.5 0.0 all-gather.4.cloned.1.call-start
  6.5 4.1 copy.11
  10.6 0.0 all-gather.4.cloned.1.call-update
  10.6 0.0 reduce-scatter.2.cloned.1.call-start
  10.7 150.9 %all-gather.4.cloned.1.call-done = bf16[256,16384]{0,1:T(8,128)(2,1)} async-done(((bf16[256,4096]{0,1:T(8,128)(2,1)}), bf16[256,16384]{0,1:T(8,128)(2,1)}) %all-gather.4.cloned.1.call-update) | async-done | bytes 8388624 | tf_op jit(solution)/shard_map/all_gather | solution.py:25
  161.6 99.4 %all_to_all.38 = bf16[256,4,4096]{0,2,1:T(8,128)(2,1)} all-to-all(bf16[256,4,4096]{0,2,1:T(8,128)(2,1)} %bitcast.17), channel_id=1, replica_groups=mesh['grp'=2,'row'=4,'col'=4] {'row'}, dimensions={1} | all-to-all | bytes 16777216 | tf_op jit(solution)/shard_map/all_to_all | solution.py:26
  261.0 11.4 %copy.12 = bf16[4,256,4096]{2,1,0:T(8,128)(2,1)} copy(bf16[4,256,4096]{1,2,0:T(8,128)(2,1)} %bitcast.15) | data formatting | bytes 16777216 | tf_op jit(solution)/shard_map/all_to_all | solution.py:26
  272.5 43.0 %fusion.2 = f32[1024,4096]{1,0:T(8,128)} fusion(bf16[1024,4096]{1,0:T(8,128)(2,1)} %bitcast.18, bf16[4096,4096]{1,0:T(8,128)(2,1)} %param.6), kind=kOutput, calls=%fused_computation.13 | convolution fusion | flops 34359738368 | bytes 58720256 | tf_op jit(solution)/shard_map/dot_general | solution.py:28
  315.5 0.0 reduce-scatter.2.cloned.1.call-update
  315.5 0.0 all-gather.6.cloned.1.call-start
  315.6 123.8 %reduce-scatter.2.cloned.1.call-done = f32[256,4096]{1,0:T(8,128)} async-done(((f32[1024,4096]{1,0:T(8,128)}), f32[256,4096]{1,0:T(8,128)}) %reduce-scatter.2.cloned.1.call-update) | async-done | bytes 4194320 | tf_op jit(solution)/shard_map/reduce_scatter | solution.py:27
  439.4 4.1 add_convert_fusion
  443.4 0.0 all-gather.6.cloned.1.call-update
  443.5 0.0 all-gather.8.cloned.1.call-start
  443.5 0.5 all-gather.8.cloned.1.call-update
  444.1 150.1 %all-gather.6.cloned.1.call-done = bf16[256,16384]{1,0:T(8,128)(2,1)} async-done(((bf16[256,4096]{1,0:T(8,128)(2,1)}), bf16[256,16384]{1,0:T(8,128)(2,1)}) %all-gather.6.cloned.1.call-update) | async-done | bytes 8388624 | tf_op jit(solution)/shard_map/all_gather | solution.py:35
  594.2 8.4 %copy.16 = bf16[32,4,8,4096]{3,2,0,1:T(8,128)(2,1)} copy(bf16[32,4,8,4096]{3,2,1,0:T(8,128)(2,1)} %bitcast.16) | data formatting | bytes 16777216 | tf_op jit(solution)/shard_map/all_to_all | solution.py:36
  602.6 6.9 all-to-all-start.1
  609.5 0.2 select_reduce_fusion.3
  609.8 0.0 copy-done.3
  609.8 3.1 select_reduce_fusion.1
  612.9 76.9 %all-gather.8.cloned.1.call-done = bf16[1024,4096]{1,0:T(8,128)(2,1)} async-done(((bf16[256,4096]{1,0:T(8,128)(2,1)}), bf16[1024,4096]{1,0:T(8,128)(2,1)}) %all-gather.8.cloned.1.call-update) | async-done | bytes 8388624 | tf_op jit(solution)/shard_map/all_gather | solution.py:39
  689.8 49.7 %all-to-all-done.1 = bf16[256,4,4096]{2,0,1:T(8,128)(2,1)} async-done(((bf16[256,4,4096]{2,0,1:T(8,128)(2,1)}), bf16[256,4,4096]{2,0,1:T(8,128)(2,1)}, u32[]{:S(2)}, u32[]{:S(2)}) %all-to-all-start.1) | async-done | bytes 8388640 | tf_op jit(solution)/shard_map/all_to_all | solution.py:36
  739.5 47.6 %divide_convert_fusion = bf16[4096,4096]{1,0:T(8,128)(2,1)} fusion(bf16[1024,4096]{1,0:T(8,128)(2,1)} %bitcast.4, bf16[1024,4096]{1,0:T(8,128)(2,1)} %all-gather.8.cloned.1.call-done, f32[4096]{0:T(1024)S(1)} %sub.15, f32[4096]{0:T(1024)S(1)} %sub.14), kind=kOutput, calls=%fused_computation | convolution fusion | flops 34426847232 | bytes 50364416 | tf_op jit(solution)/shard_map/dot_general | solution.py:37
  (12 shorter events, 0.0 us)
Async XLA Ops:
  6.5 155.1 %all-gather.4.cloned.1.call-start = ((), (), s32[]{:S(2)}) async-start(), calls=%async_computation.3 | async-start | bytes 10485760 | tf_op jit(solution)/shard_map/all_gather | solution.py:25
  10.6 428.7 %reduce-scatter.2.cloned.1.call-start = ((), (), s32[]{:S(2)}) async-start(), calls=%async_computation.4 | async-start | bytes 20971520 | tf_op jit(solution)/shard_map/reduce_scatter | solution.py:27
  315.5 123.8 %copy-start = (bf16[256,4096]{1,0:T(8,128)(2,1)S(1)}, bf16[256,4096]{1,0:T(8,128)(2,1)}, u32[]{:S(2)}) copy-start(bf16[256,4096]{1,0:T(8,128)(2,1)} %param.7) | copy-start | bytes 6291460
  315.5 278.7 %all-gather.6.cloned.1.call-start = ((), (), s32[]{:S(2)}) async-start(), calls=%async_computation.5 | async-start | bytes 10485760 | tf_op jit(solution)/shard_map/all_gather | solution.py:35
  443.5 246.3 %all-gather.8.cloned.1.call-start = ((), (), s32[]{:S(2)}) async-start(), calls=%async_computation.6 | async-start | bytes 10485760 | tf_op jit(solution)/shard_map/all_gather | solution.py:39
  602.6 6.9 copy-start.1
  602.6 6.9 copy-start.2
  602.6 6.9 copy-start.4
  602.6 7.2 copy-start.3
  602.6 136.9 %all-to-all-start.1 = ((bf16[256,4,4096]{2,0,1:T(8,128)(2,1)}), bf16[256,4,4096]{2,0,1:T(8,128)(2,1)}, u32[]{:S(2)}, u32[]{:S(2)}) async-start(bf16[256,4,4096]{2,0,1:T(8,128)(2,1)} %bitcast.14), calls=%async_computation.2 | async-start | bytes 16777216 | tf_op jit(solution)/shard_map/all_to_all | solution.py:36
Sparse Core Ops, SparseCore 0:
  10.7 150.8 all-gather.3
  315.7 123.6 reduce-scatter.1
  443.6 150.5 all-gather.5
  595.7 94.1 all-gather.7
where the time goes:
time: 797 us; the launch traced here: 794 us
  waiting for transfers between devices  552 us (69%)
  blocking collectives  99.4 us (12%)
  matrix products  90.6 us (11%)
  local copies, waits for them, and re-layouts  23.9 us (3%)
  between operations  13.2 us (2%)
    all_gather x1, waiting for transfers between devices, local(): all_pairs = lax.all_gather(cholesky, 'col', axis=1, tiled=True)  151 us
    all_gather x1, waiting for transfers between devices, local(): ydress_pairs = lax.all_gather(ydress, 'col', axis=1, tiled=True)  150 us
    reduce_scatter x1, waiting for transfers between devices, local(): lax.psum_scatter(jnp.dot(chol_rows, amplitudes, preferred_element_type=jn...  124 us
    all_to_all x1, blocking collectives, local(): lax.all_to_all(all_pairs, 'row', split_axis=1, concat_axis=0, tiled=True)  99.4 us
    all_gather x1, waiting for transfers between devices, local(): lax.all_gather(ydress, 'row', axis=0, tiled=True)  76.9 us
    all_to_all x1, waiting for transfers between devices, local(): lax.all_to_all(ydress_pairs, 'row', split_axis=1, concat_axis=0, tiled=True)  49.7 us
    dot_general x1, matrix products, local(): lax.dot_general(ydress_rows, lax.all_gather(ydress, 'row', axis=0, tiled=...  47.6 us
    dot_general x1, matrix products, local(): jnp.dot(chol_rows, amplitudes, preferred_element_type=jnp.float32)  43 us
  transfers between devices with their start and end apart: 5, of which 5 were waited for; matrix products, arithmetic and copies ran while one was open for 1% of the time, Pallas kernels for 0%

commit v1 on v0

--- a/solution.py
+++ b/solution.py
@@ -1,7 +1,13 @@
 import jax
 import jax.numpy as jnp
 from jax import lax
+from jax.experimental import pallas as pl
+from jax.experimental.pallas import tpu as pltpu
 from jax.sharding import PartitionSpec as P
+
+AXES = ("row", "col")
+BF16 = jnp.bfloat16
+F32 = jnp.float32
 
 
 def pair_gaps(occ_index, vir_index, eps_occ, eps_vir, begin_pair, pair_count):
@@ -18,19 +24,19 @@
     return vir_energy - occ_energy
 
 
-def local(amplitudes, cholesky, occ_index, vir_index, eps_occ, eps_vir):
+def general(amplitudes, cholesky, occ_index, vir_index, eps_occ, eps_vir):
     row_position = lax.axis_index("row")
     col_position = lax.axis_index("col")
     rows_block, cols_block = amplitudes.shape
     all_pairs = lax.all_gather(cholesky, "col", axis=1, tiled=True)
     chol_rows = lax.all_to_all(all_pairs, "row", split_axis=1, concat_axis=0, tiled=True)
     dressed = lax.psum_scatter(
-        jnp.dot(chol_rows, amplitudes, preferred_element_type=jnp.float32),
+        jnp.dot(chol_rows, amplitudes, preferred_element_type=F32),
         "row",
         scatter_dimension=0,
         tiled=True,
     )
-    ydress = (cholesky.astype(jnp.float32) + dressed).astype(jnp.bfloat16)
+    ydress = (cholesky.astype(F32) + dressed).astype(BF16)
     contract = (((0,), (0,)), ((), ()))
     ydress_pairs = lax.all_gather(ydress, "col", axis=1, tiled=True)
     ydress_rows = lax.all_to_all(ydress_pairs, "row", split_axis=1, concat_axis=0, tiled=True)
@@ -38,7 +44,7 @@
         ydress_rows,
         lax.all_gather(ydress, "row", axis=0, tiled=True),
         contract,
-        preferred_element_type=jnp.float32,
+        preferred_element_type=F32,
     )
     gap_rows = pair_gaps(
         occ_index, vir_index, eps_occ, eps_vir, row_position * rows_block, rows_block
@@ -46,12 +52,214 @@
     gap_cols = pair_gaps(
         occ_index, vir_index, eps_occ, eps_vir, col_position * cols_block, cols_block
     )
-    return (-gram / (gap_rows[:, None] + gap_cols[None, :])).astype(jnp.bfloat16)
+    return (-gram / (gap_rows[:, None] + gap_cols[None, :])).astype(BF16)
+
+
+SIDE = 4
+VMEM = 50 * 2**20
+ANY = pl.BlockSpec(memory_space=pl.ANY)
+
+
+def dev(r, z):
+    return r * SIDE + z
+
+
+def plane(e):
+    return [(dev(r, z), dev(r ^ e, z)) for r in range(SIDE) for z in range(SIDE)]
+
+
+def deal(i):
+    return [(dev(q, b), dev(b, q ^ i)) for q in range(SIDE) for b in range(SIDE)]
+
+
+def send(a, edges, name):
+    with jax.named_scope(name):
+        return lax.ppermute(a, AXES, edges)
+
+
+def after(a, *done):
+    return lax.optimization_barrier((a,) + done)[0]
+
+
+def chunk_sizes(depth):
+    return [depth // 2] * 2
+
+
+def fetch(turn, dealt, dst, sem):
+    kq = dealt[0].shape[0]
+    for k in range(SIDE):
+        @pl.when(turn == k)
+        def _(k=k):
+            copies = [
+                pltpu.make_async_copy(dealt[e ^ k], dst.at[pl.ds(e * kq, kq), :], sem.at[e]) for e in range(SIDE)
+            ]
+            for c in copies:
+                c.start()
+            for c in copies:
+                c.wait()
+
+
+def pick(turn, dealt):
+    kq, width = dealt[0].shape
+
+    def kernel(turn_ref, *rest):
+        fetch(turn_ref[0], rest[:SIDE], rest[SIDE], rest[SIDE + 1])
+
+    return pl.pallas_call(
+        kernel,
+        out_shape=jax.ShapeDtypeStruct((SIDE * kq, width), BF16),
+        in_specs=[pl.BlockSpec(memory_space=pltpu.SMEM)] + [ANY] * SIDE,
+        out_specs=pl.BlockSpec(memory_space=pltpu.VMEM),
+        scratch_shapes=[pltpu.SemaphoreType.DMA((SIDE,))],
+        compiler_params=pltpu.CompilerParams(vmem_limit_bytes=VMEM),
+        cost_estimate=pl.CostEstimate(flops=0, bytes_accessed=4 * SIDE * kq * width, transcendentals=0),
+        name="pick",
+    )(turn, *dealt)
+
+
+def dress(turn, dealt, amplitudes):
+    kq = dealt[0].shape[0]
+    depth, width = amplitudes.shape
+    tile = min(512, width)
+
+    def kernel(turn_ref, t_ref, *rest):
+        dealt_refs = rest[:SIDE]
+        keep, give, rows, sem = rest[SIDE:]
+
+        @pl.when(pl.program_id(0) == 0)
+        def _():
+            fetch(turn_ref[0], dealt_refs, rows, sem)
+
+        part = jnp.dot(rows[...], t_ref[...], preferred_element_type=F32)
+        keep[:kq, :] = part[:kq]
+        give[:kq, :] = part[kq:2 * kq].astype(give.dtype)
+        keep[kq:, :] = part[2 * kq:3 * kq]
+        give[kq:, :] = part[3 * kq:].astype(give.dtype)
+
+    return pl.pallas_call(
+        kernel,
+        grid=(width // tile,),
+        out_shape=[jax.ShapeDtypeStruct((2 * kq, width), F32), jax.ShapeDtypeStruct((2 * kq, width), BF16)],
+        in_specs=[pl.BlockSpec(memory_space=pltpu.SMEM), pl.BlockSpec((depth, tile), lambda j: (0, j))] + [ANY] * SIDE,
+        out_specs=[pl.BlockSpec((2 * kq, tile), lambda j: (0, j))] * 2,
+        scratch_shapes=[pltpu.VMEM((SIDE * kq, depth), BF16), pltpu.SemaphoreType.DMA((SIDE,))],
+        compiler_params=pltpu.CompilerParams(vmem_limit_bytes=VMEM),
+        cost_estimate=pl.CostEstimate(
+            flops=2 * SIDE * kq * depth * width,
+            bytes_accessed=2 * depth * width + 20 * kq * width,
+            transcendentals=0),
+        name="dress",
+    )(turn, amplitudes, *dealt)
+
+
+def gram(rows, cols, gap_rows, gap_cols, partial):
+    n = len(rows)
+    height, width = rows[0].shape[1], cols[0].shape[1]
+    depth = sum(a.shape[0] for a in rows)
+    tile = min(512, height)
+    strip = min(2048, width)
+
+    def kernel(*refs):
+        lhs, rhs = refs[:n], refs[n:2 * n]
+        gr, gc = refs[2 * n:2 * n + 2]
+        old = refs[2 * n + 2] if partial is not None else None
+        out = refs[-1]
+        for j in range(width // strip):
+            at = pl.ds(j * strip, strip)
+            total = None
+            for a, b in zip(lhs, rhs):
+                term = lax.dot_general(a[...], b[:, at], (((0,), (0,)), ((), ())), preferred_element_type=F32)
+                total = term if total is None else total + term
+            if old is not None:
+                gap = gr[...] + gc[:, at]
+                inverse = pl.reciprocal(gap, approx=True)
+                inverse = inverse * (gap * inverse - 2.0)
+                total = (total + old[:, at].astype(F32)) * inverse
+            out[:, at] = total.astype(BF16)
+
+    whole = [pl.BlockSpec(a.shape, lambda i: (0, 0)) for a in cols]
+    tall = [pl.BlockSpec((a.shape[0], tile), lambda i: (0, i)) for a in rows]
+    specs = tall + whole + [pl.BlockSpec((tile, 1), lambda i: (i, 0)), pl.BlockSpec((1, width), lambda i: (0, 0))]
+    args = list(rows) + list(cols) + [gap_rows[:, None], gap_cols[None, :]]
+    alias = {}
+    if partial is not None:
+        specs.append(pl.BlockSpec((tile, width), lambda i: (i, 0)))
+        alias = {len(args): 0}
+        args.append(partial)
+    return pl.pallas_call(
+        kernel,
+        grid=(height // tile,),
+        out_shape=jax.ShapeDtypeStruct((height, width), BF16),
+        in_specs=specs,
+        out_specs=pl.BlockSpec((tile, width), lambda i: (i, 0)),
+        input_output_aliases=alias,
+        compiler_params=pltpu.CompilerParams(vmem_limit_bytes=VMEM),
+        cost_estimate=pl.CostEstimate(
+            flops=2 * depth * height * width,
+            bytes_accessed=(4 if partial is not None else 2) * height * width,
+            transcendentals=0),
+        name="gram",
+    )(*args)
+
+
+def four(amplitudes, cholesky, occ_index, vir_index, eps_occ, eps_vir):
+    r = lax.axis_index("row")
+    z = lax.axis_index("col")
+    rows_block, cols_block = amplitudes.shape
+    gap_rows = pair_gaps(occ_index, vir_index, eps_occ, eps_vir, r * rows_block, rows_block)
+    gap_cols = pair_gaps(occ_index, vir_index, eps_occ, eps_vir, z * cols_block, cols_block)
+    turn = (r ^ z).astype(jnp.int32).reshape(1)
+    cat = lambda *a: jnp.concatenate(a, axis=0)
+    sizes = chunk_sizes(cholesky.shape[0])
+    n = len(sizes)
+    own = [lax.slice_in_dim(cholesky, sum(sizes[:c]), sum(sizes[:c + 1]), axis=0) for c in range(n)]
+
+    previous = [()] * SIDE
+
+    def dealt(a, name, gate=()):
+        got = []
+        for i in range(SIDE):
+            waits = previous[i] + (tuple(gate) if i == SIDE - 1 else ())
+            got.append(send(after(a, *waits), deal(i), "%s_%d" % (name, i)))
+        previous[:] = [(g,) for g in got]
+        return got
+
+    chol, sums, lean, other = [], [], [], []
+    rows, cols = [], []
+
+    def start_sums(c):
+        keep, give = dress(after(turn, *other[-1:]), chol[c], amplitudes)
+        both = keep + send(give, plane(1), "sum_core_%d" % c).astype(F32)
+        mine = both[:sizes[c]] + own[c].astype(F32)
+        sums.append((mine, both[sizes[c]:]))
+        lean.append(cat(*sums[c]).astype(BF16))
+        other.append(send(after(lean[c], *other[-1:]), plane(2), "sum_x_%d" % c))
+
+    for c in range(n):
+        chol.append(dealt(own[c], "factors_%d" % c, lean[-1:] if c >= 2 else ()))
+        if c >= 1:
+            start_sums(c - 1)
+    start_sums(n - 1)
+
+    early = None
+    for c in range(n):
+        kq = sizes[c]
+        y0 = (sums[c][0] + other[c][kq:].astype(F32)).astype(BF16)
+        y2 = (sums[c][1] + other[c][:kq].astype(F32)).astype(BF16)
+        core = send(cat(y0, y2), plane(1), "y_core_%d" % c)
+        cols.append(cat(y0, core[:kq], y2, core[kq:]))
+        if c == n - 1:
+            early = gram(rows, cols[:c], gap_rows, gap_cols, None)
+        gate = (early,) if c == n - 1 else lean[-1:]
+        rows.append(pick(turn, dealt(y0, "dressed_%d" % c, gate)))
+    return gram(rows[n - 1:], cols[n - 1:], gap_rows, gap_cols, early)
 
 
 def solution(mesh):
+    shape = dict(mesh.shape)
+    body = four if shape["row"] == SIDE and shape["col"] == SIDE else general
     return jax.shard_map(
-        local,
+        body,
         mesh=mesh,
         in_specs=(
             P(("grp", "row"), "col"),

time: 797 us -> 508 us (0.64)
  waiting for transfers between devices: 552 us -> 285 us
  Pallas kernels: 0 us -> 113 us
  blocking collectives: 99.4 us -> 0 us
  matrix products: 90.6 us -> 0 us
  starting transfers between devices: 7.03 us -> 75.3 us
  other arithmetic: 7.47 us -> 25.8 us
  local copies, waits for them, and re-layouts: 23.9 us -> 7.62 us
  between operations: 13.2 us -> 0.35 us
    all_gather x3 -> x0, waiting for transfers between devices: 378 us -> none  [the longest x1 151 us: local(): all_pairs = lax.all_gather(cholesky, 'col', axis=1, tiled=True)]
    ppermute x0 -> x22, waiting for transfers between devices: none -> 285 us  [send(): return lax.ppermute(a, AXES, edges)]
    reduce_scatter x1 -> x0, waiting for transfers between devices: 124 us -> none  [local(): lax.psum_scatter(jnp.dot(chol_rows, amplitudes, preferred_element_type=jn...]
    pallas_call x0 -> x6, Pallas kernels: none -> 113 us  [the longest x2 58 us: gram(): pl.pallas_call(kernel, grid=(height // tile,), out_shape=jax.ShapeDtypeSt...]
    all_to_all x1 -> x0, blocking collectives: 99.4 us -> none  [local(): lax.all_to_all(all_pairs, 'row', split_axis=1, concat_axis=0, tiled=True)]
    dot_general x2 -> x0, matrix products: 90.6 us -> none  [the longest x1 47.6 us: local(): lax.dot_general(ydress_rows, lax.all_gather(ydress, 'row', axis=0, tiled=...]
    ppermute x0 -> x22, starting transfers between devices: none -> 75.3 us  [send(): return lax.ppermute(a, AXES, edges)]
    all_to_all x1 -> x0, waiting for transfers between devices: 49.7 us -> none  [local(): lax.all_to_all(ydress_pairs, 'row', split_axis=1, concat_axis=0, tiled=True)]
  transfers between devices with their start and end apart: 5 -> 22, of which waited for: 5 -> 13; matrix products, arithmetic and copies ran while one was open for 1% -> 3% of each run, Pallas kernels for 0% -> 6%
where the time goes in v1:
time: 508 us; the launch traced here: 507 us
  waiting for transfers between devices  285 us (56%)
  Pallas kernels  113 us (22%)
  starting transfers between devices  75.3 us (15%)
  other arithmetic  25.8 us (5%)
  local copies, waits for them, and re-layouts  7.62 us (2%)
    ppermute x22, waiting for transfers between devices, send(): return lax.ppermute(a, AXES, edges)  285 us
    ppermute x22, starting transfers between devices, send(): return lax.ppermute(a, AXES, edges)  75.3 us
    pallas_call x2, Pallas kernels, gram(): pl.pallas_call(kernel, grid=(height // tile,), out_shape=jax.ShapeDtypeSt...  58 us
    pallas_call x2, Pallas kernels, dress(): pl.pallas_call(kernel, grid=(width // tile,), out_shape=[jax.ShapeDtypeSt...  47.8 us
    concatenate x6, other arithmetic, four(): cat = lambda *a: jnp.concatenate(a, axis=0)  11.7 us
  transfers between devices with their start and end apart: 22, of which 13 were waited for; matrix products, arithmetic and copies ran while one was open for 3% of the time, Pallas kernels for 6%

profile of v1, /device:TPU:6, one launch (start us, length us, event | category | flops | bytes accessed | tf_op | source)
XLA Modules:
  0.0 506.7 jit_solution(1257647759815350594)
XLA Ops:
  0.0 3.1 fusion.4
  8.1 3.6 collective-permute-start
  11.7 62.6 %collective-permute-done.3.rest_3_ = bf16[128,4096]{1,0:T(8,128)(2,1)} collective-permute-done((bf16[128,4096]{1,0:T(8,128)(2,1)}, bf16[128,4096]{1,0:T(8,128)(2,1)}, u32[]{:S(2)}, u32[]{:S(2)}) %collective-permute-start.3) | collective-permute-done | bytes 1048608 | tf_op jit(solution)/shard_map/factors_0_3/ppermute | solution.py:77
  74.2 22.8 %collective-permute-done.2.rest_2_ = bf16[128,4096]{1,0:T(8,128)(2,1)S(1)} collective-permute-done((bf16[128,4096]{1,0:T(8,128)(2,1)}, bf16[128,4096]{1,0:T(8,128)(2,1)S(1)}, u32[]{:S(2)}, u32[]{:S(2)}) %collective-permute-start.2) | collective-permute-done | bytes 1048608 | tf_op jit(solution)/shard_map/factors_0_2/ppermute | solution.py:77
  97.1 3.6 collective-permute-done.rest_0_
  100.7 23.9 %dress.2 = (f32[256,4096]{1,0:T(8,128)}, bf16[256,4096]{1,0:T(8,128)(2,1)}) custom-call(s32[1]{0:T(128)} %bitcast.turn_ref, bf16[4096,4096]{1,0:T(8,128)(2,1)} %t_ref.3, bf16[128,4096]{1,0:T(8,128)(2,1)S(1)} %collective-permute-done.rest_0_, bf16[128,4096]{1,0:T(8,128)(2,1)S(1)} %collective-permute-done.1.rest_1_, ...), custom_call_target="tpu_custom_call" | custom-call | flops 17179869184 | bytes 44040192 | tf_op jit(solution)/shard_map/dress/pallas_call | solution.py:139
  124.7 4.4 collective-permute-done.4
  140.4 81.3 %collective-permute-done.5 = bf16[256,4096]{1,0:T(8,128)(2,1)S(1)} collective-permute-done((bf16[256,4096]{1,0:T(8,128)(2,1)S(1)}, bf16[256,4096]{1,0:T(8,128)(2,1)S(1)}, u32[]{:S(2)}, u32[]{:S(2)}) %collective-permute-start.5) | collective-permute-done | bytes 2097184 | tf_op jit(solution)/shard_map/sum_x_0/ppermute | solution.py:77
  221.7 5.5 %collective-permute-done.8.rest_2_ = bf16[128,4096]{1,0:T(8,128)(2,1)S(1)} collective-permute-done((bf16[128,4096]{1,0:T(8,128)(2,1)S(1)}, bf16[128,4096]{1,0:T(8,128)(2,1)S(1)}, u32[]{:S(2)}, u32[]{:S(2)}) %collective-permute-start.8) | collective-permute-done | bytes 1048608 | tf_op jit(solution)/shard_map/factors_1_2/ppermute | solution.py:77
  229.1 23.9 %dress.3 = (f32[256,4096]{1,0:T(8,128)}, bf16[256,4096]{1,0:T(8,128)(2,1)}) custom-call(s32[1]{0:T(128)} %bitcast.turn_ref, bf16[4096,4096]{1,0:T(8,128)(2,1)} %t_ref.3, bf16[128,4096]{1,0:T(8,128)(2,1)S(1)} %collective-permute-done.6.rest_0_, bf16[128,4096]{1,0:T(8,128)(2,1)S(1)} %collective-permute-done.7.rest_1_, ...), custom_call_target="tpu_custom_call" | custom-call | flops 17179869184 | bytes 44040192 | tf_op jit(solution)/shard_map/dress/pallas_call | solution.py:139
  253.1 4.4 collective-permute-done.10
  266.9 4.0 collective-permute-start.12
  275.6 37.5 %collective-permute-done.18.rest_3_ = bf16[128,4096]{1,0:T(8,128)(2,1)S(1)} collective-permute-done((bf16[128,4096]{1,0:T(8,128)(2,1)}, bf16[128,4096]{1,0:T(8,128)(2,1)S(1)}, u32[]{:S(2)}, u32[]{:S(2)}) %collective-permute-start.18) | collective-permute-done | bytes 1048608 | tf_op jit(solution)/shard_map/dressed_0_3/ppermute | solution.py:77
  313.1 41.6 %collective-permute-start.19 = (bf16[256,4096]{1,0:T(8,128)(2,1)}, bf16[256,4096]{1,0:T(8,128)(2,1)}, u32[]{:S(2)}, u32[]{:S(2)}) collective-permute-start(bf16[256,4096]{1,0:T(8,128)(2,1)} %pad_maximum_fusion.4), channel_id=1, source_target_pairs={{0,4},{1,5},{2,6},{3,7},{4,0},{5,1},{6,2},{7,3},{8,12},{9,13},{10,... | collective-permute-start | bytes 6291464 | tf_op jit(solution)/shard_map/y_core_0/ppermute | solution.py:77
  354.9 3.1 select_reduce_fusion
  360.4 4.1 pick.2.refs_0_
  366.8 3.5 collective-permute-start.13
  376.0 3.3 pad_maximum_fusion.refs_1_
  379.3 23.5 %gram.2.refs_4_ = bf16[4096,4096]{1,0:T(8,128)(2,1)} custom-call(bf16[512,4096]{1,0:T(8,128)(2,1)} %pick.2.refs_0_, bf16[512,4096]{1,0:T(8,128)(2,1)} %pad_maximum_fusion.refs_1_, f32[4096,1]{1,0:T(8,128)S(1)} %copy.10.refs_2_, f32[1,4096]{1,0:T(1,128)S(1)} %bitcast.3), custom_call_target="tpu_custom_call" | custom-call | flops 17179869184 | bytes 33554432 | tf_op jit(solution)/shard_map/gram/pallas_call | solution.py:189
  402.8 3.6 collective-permute-start.20
  406.4 34.9 %collective-permute-done.13.rest_0_ = bf16[128,4096]{1,0:T(8,128)(2,1)S(1)} collective-permute-done((bf16[128,4096]{1,0:T(8,128)(2,1)S(1)}, bf16[128,4096]{1,0:T(8,128)(2,1)S(1)}, u32[]{:S(2)}, u32[]{:S(2)}) %collective-permute-start.13) | collective-permute-done | bytes 1048608 | tf_op jit(solution)/shard_map/dressed_1_0/ppermute | solution.py:77
  441.3 22.7 %collective-permute-done.15.rest_1_ = bf16[128,4096]{1,0:T(8,128)(2,1)S(1)} collective-permute-done((bf16[128,4096]{1,0:T(8,128)(2,1)S(1)}, bf16[128,4096]{1,0:T(8,128)(2,1)S(1)}, u32[]{:S(2)}, u32[]{:S(2)}) %collective-permute-start.15) | collective-permute-done | bytes 1048608 | tf_op jit(solution)/shard_map/dressed_1_1/ppermute | solution.py:77
  466.5 3.3 pick.3.refs_0_
  472.3 34.5 %gram.3 = bf16[4096,4096]{1,0:T(8,128)(2,1)} custom-call(bf16[512,4096]{1,0:T(8,128)(2,1)} %pick.3.refs_0_, bf16[512,4096]{1,0:T(8,128)(2,1)} %pad_maximum_fusion.1.refs_1_, f32[4096,1]{1,0:T(8,128)S(1)} %copy.10.refs_2_, f32[1,4096]{1,0:T(1,128)S(1)} %bitcast.4, bf16[4096,4096]{1,0:T(8,128)(2,1)} %gram.2.refs_4_), custom_call_target="tpu_custom_call", output_to_operand_aliasing={{}: (4, {})} | custom-call | flops 17179869184 | bytes 67108864 | tf_op jit(solution)/shard_map/gram/pallas_call | solution.py:189
  (76 shorter events, 47.8 us)
Async XLA Ops:
  3.1 71.2 %collective-permute-start.3 = (bf16[128,4096]{1,0:T(8,128)(2,1)}, bf16[128,4096]{1,0:T(8,128)(2,1)}, u32[]{:S(2)}, u32[]{:S(2)}) collective-permute-start(bf16[128,4096]{1,0:T(8,128)(2,1)} %get-tuple-element.55), channel_id=1, source_target_pairs={{0,3},{1,7},{2,11},{3,15},{4,2},{5,6},{6,10},{7,14},{8,1},{9,5},{1... | collective-permute-start | bytes 3145736 | tf_op jit(solution)/shard_map/factors_0_3/ppermute | solution.py:77
  4.6 92.4 %collective-permute-start.2 = (bf16[128,4096]{1,0:T(8,128)(2,1)}, bf16[128,4096]{1,0:T(8,128)(2,1)S(1)}, u32[]{:S(2)}, u32[]{:S(2)}) collective-permute-start(bf16[128,4096]{1,0:T(8,128)(2,1)} %get-tuple-element.55), channel_id=1, source_target_pairs={{0,2},{1,6},{2,10},{3,14},{4,3},{5,7},{6,11},{7,15},{8,0},{9,4},{1... | collective-permute-start | bytes 3145736 | tf_op jit(solution)/shard_map/factors_0_2/ppermute | solution.py:77
  7.2 89.8 %collective-permute-start.1 = (bf16[128,4096]{1,0:T(8,128)(2,1)}, bf16[128,4096]{1,0:T(8,128)(2,1)S(1)}, u32[]{:S(2)}, u32[]{:S(2)}) collective-permute-start(bf16[128,4096]{1,0:T(8,128)(2,1)} %get-tuple-element.55), channel_id=1, source_target_pairs={{0,1},{1,5},{2,9},{3,13},{4,0},{5,4},{6,8},{7,12},{8,3},{9,7},{10,... | collective-permute-start | bytes 3145736 | tf_op jit(solution)/shard_map/factors_0_1/ppermute | solution.py:77
  8.1 92.6 %collective-permute-start = (bf16[128,4096]{1,0:T(8,128)(2,1)}, bf16[128,4096]{1,0:T(8,128)(2,1)S(1)}, u32[]{:S(2)}, u32[]{:S(2)}) collective-permute-start(bf16[128,4096]{1,0:T(8,128)(2,1)} %get-tuple-element.55), channel_id=1, source_target_pairs={{0,0},{1,4},{2,8},{3,12},{4,1},{5,5},{6,9},{7,13},{8,2},{9,6},{10,... | collective-permute-start | bytes 3145736 | tf_op jit(solution)/shard_map/factors_0_0/ppermute | solution.py:77
  124.6 4.4 collective-permute-start.4
  132.7 89.0 %collective-permute-start.5 = (bf16[256,4096]{1,0:T(8,128)(2,1)S(1)}, bf16[256,4096]{1,0:T(8,128)(2,1)S(1)}, u32[]{:S(2)}, u32[]{:S(2)}) collective-permute-start(bf16[256,4096]{1,0:T(8,128)(2,1)S(1)} %pad_maximum_fusion.2), channel_id=1, source_target_pairs={{0,8},{1,9},{2,10},{3,11},{4,12},{5,13},{6,14},{7,15},{8,0},{9,1},... | collective-permute-start | bytes 6291464 | tf_op jit(solution)/shard_map/sum_x_0/ppermute | solution.py:77
  133.5 88.3 %collective-permute-start.9 = (bf16[128,4096]{1,0:T(8,128)(2,1)S(1)}, bf16[128,4096]{1,0:T(8,128)(2,1)S(1)}, u32[]{:S(2)}, u32[]{:S(2)}) collective-permute-start(bf16[128,4096]{1,0:T(8,128)(2,1)S(1)} %copy-done.8), channel_id=1, source_target_pairs={{0,3},{1,7},{2,11},{3,15},{4,2},{5,6},{6,10},{7,14},{8,1},{9,5},{1... | collective-permute-start | bytes 3145736 | tf_op jit(solution)/shard_map/factors_1_3/ppermute | solution.py:77
  135.5 91.8 %collective-permute-start.8 = (bf16[128,4096]{1,0:T(8,128)(2,1)S(1)}, bf16[128,4096]{1,0:T(8,128)(2,1)S(1)}, u32[]{:S(2)}, u32[]{:S(2)}) collective-permute-start(bf16[128,4096]{1,0:T(8,128)(2,1)S(1)} %copy-done.8), channel_id=1, source_target_pairs={{0,2},{1,6},{2,10},{3,14},{4,3},{5,7},{6,11},{7,15},{8,0},{9,4},{1... | collective-permute-start | bytes 3145736 | tf_op jit(solution)/shard_map/factors_1_2/ppermute | solution.py:77
  135.5 91.7 %collective-permute-start.7 = (bf16[128,4096]{1,0:T(8,128)(2,1)S(1)}, bf16[128,4096]{1,0:T(8,128)(2,1)S(1)}, u32[]{:S(2)}, u32[]{:S(2)}) collective-permute-start(bf16[128,4096]{1,0:T(8,128)(2,1)S(1)} %copy-done.8), channel_id=1, source_target_pairs={{0,1},{1,5},{2,9},{3,13},{4,0},{5,4},{6,8},{7,12},{8,3},{9,7},{10,... | collective-permute-start | bytes 3145736 | tf_op jit(solution)/shard_map/factors_1_1/ppermute | solution.py:77
  138.5 90.6 %collective-permute-start.6 = (bf16[128,4096]{1,0:T(8,128)(2,1)S(1)}, bf16[128,4096]{1,0:T(8,128)(2,1)S(1)}, u32[]{:S(2)}, u32[]{:S(2)}) collective-permute-start(bf16[128,4096]{1,0:T(8,128)(2,1)S(1)} %copy-done.8), channel_id=1, source_target_pairs={{0,0},{1,4},{2,8},{3,12},{4,1},{5,5},{6,9},{7,13},{8,2},{9,6},{10,... | collective-permute-start | bytes 3145736 | tf_op jit(solution)/shard_map/factors_1_0/ppermute | solution.py:77
  253.0 4.4 collective-permute-start.10
  262.7 92.0 %copy-start.12 = (f32[32]{0:T(128)S(1)}, f32[32]{0:T(128)}, u32[]{:S(2)}) copy-start(f32[32]{0:T(128)} %param.10) | copy-start | bytes 388
  262.7 92.2 %copy-start.11 = (f32[512]{0:T(512)S(1)}, f32[512]{0:T(512)}, u32[]{:S(2)}) copy-start(f32[512]{0:T(512)} %param.11) | copy-start | bytes 6148
  264.3 100.2 %collective-permute-start.11 = (bf16[256,4096]{1,0:T(8,128)(2,1)}, bf16[256,4096]{1,0:T(8,128)(2,1)}, u32[]{:S(2)}, u32[]{:S(2)}) collective-permute-start(bf16[256,4096]{1,0:T(8,128)(2,1)} %pad_maximum_fusion.3), channel_id=1, source_target_pairs={{0,8},{1,9},{2,10},{3,11},{4,12},{5,13},{6,14},{7,15},{8,0},{9,1},... | collective-permute-start | bytes 6291464 | tf_op jit(solution)/shard_map/sum_x_1/ppermute | solution.py:77
  264.3 48.8 %collective-permute-start.18 = (bf16[128,4096]{1,0:T(8,128)(2,1)}, bf16[128,4096]{1,0:T(8,128)(2,1)S(1)}, u32[]{:S(2)}, u32[]{:S(2)}) collective-permute-start(bf16[128,4096]{1,0:T(8,128)(2,1)} %get-tuple-element.39), channel_id=1, source_target_pairs={{0,3},{1,7},{2,11},{3,15},{4,2},{5,6},{6,10},{7,14},{8,1},{9,5},{1... | collective-permute-start | bytes 3145736 | tf_op jit(solution)/shard_map/dressed_0_3/ppermute | solution.py:77
  266.9 91.9 %collective-permute-start.12 = (bf16[128,4096]{1,0:T(8,128)(2,1)}, bf16[128,4096]{1,0:T(8,128)(2,1)S(1)}, u32[]{:S(2)}, u32[]{:S(2)}) collective-permute-start(bf16[128,4096]{1,0:T(8,128)(2,1)} %get-tuple-element.39), channel_id=1, source_target_pairs={{0,0},{1,4},{2,8},{3,12},{4,1},{5,5},{6,9},{7,13},{8,2},{9,6},{10,... | collective-permute-start | bytes 3145736 | tf_op jit(solution)/shard_map/dressed_0_0/ppermute | solution.py:77
  270.9 89.5 %collective-permute-start.14 = (bf16[128,4096]{1,0:T(8,128)(2,1)}, bf16[128,4096]{1,0:T(8,128)(2,1)}, u32[]{:S(2)}, u32[]{:S(2)}) collective-permute-start(bf16[128,4096]{1,0:T(8,128)(2,1)} %get-tuple-element.39), channel_id=1, source_target_pairs={{0,1},{1,5},{2,9},{3,13},{4,0},{5,4},{6,8},{7,12},{8,3},{9,7},{10,... | collective-permute-start | bytes 3145736 | tf_op jit(solution)/shard_map/dressed_0_1/ppermute | solution.py:77
  272.8 87.6 %collective-permute-start.16 = (bf16[128,4096]{1,0:T(8,128)(2,1)}, bf16[128,4096]{1,0:T(8,128)(2,1)}, u32[]{:S(2)}, u32[]{:S(2)}) collective-permute-start(bf16[128,4096]{1,0:T(8,128)(2,1)} %get-tuple-element.39), channel_id=1, source_target_pairs={{0,2},{1,6},{2,10},{3,14},{4,3},{5,7},{6,11},{7,15},{8,0},{9,4},{1... | collective-permute-start | bytes 3145736 | tf_op jit(solution)/shard_map/dressed_0_2/ppermute | solution.py:77
  313.1 61.2 %collective-permute-start.19 = (bf16[256,4096]{1,0:T(8,128)(2,1)}, bf16[256,4096]{1,0:T(8,128)(2,1)}, u32[]{:S(2)}, u32[]{:S(2)}) collective-permute-start(bf16[256,4096]{1,0:T(8,128)(2,1)} %pad_maximum_fusion.4), channel_id=1, source_target_pairs={{0,4},{1,5},{2,6},{3,7},{4,0},{5,1},{6,2},{7,3},{8,12},{9,13},{10,... | collective-permute-start | bytes 6291464 | tf_op jit(solution)/shard_map/y_core_0/ppermute | solution.py:77
  366.8 74.5 %collective-permute-start.13 = (bf16[128,4096]{1,0:T(8,128)(2,1)S(1)}, bf16[128,4096]{1,0:T(8,128)(2,1)S(1)}, u32[]{:S(2)}, u32[]{:S(2)}) collective-permute-start(bf16[128,4096]{1,0:T(8,128)(2,1)S(1)} %get-tuple-element.40), channel_id=1, source_target_pairs={{0,0},{1,4},{2,8},{3,12},{4,1},{5,5},{6,9},{7,13},{8,2},{9,6},{10,... | collective-permute-start | bytes 3145736 | tf_op jit(solution)/shard_map/dressed_1_0/ppermute | solution.py:77
  370.3 93.6 %collective-permute-start.15 = (bf16[128,4096]{1,0:T(8,128)(2,1)S(1)}, bf16[128,4096]{1,0:T(8,128)(2,1)S(1)}, u32[]{:S(2)}, u32[]{:S(2)}) collective-permute-start(bf16[128,4096]{1,0:T(8,128)(2,1)S(1)} %get-tuple-element.40), channel_id=1, source_target_pairs={{0,1},{1,5},{2,9},{3,13},{4,0},{5,4},{6,8},{7,12},{8,3},{9,7},{10,... | collective-permute-start | bytes 3145736 | tf_op jit(solution)/shard_map/dressed_1_1/ppermute | solution.py:77
  372.7 91.3 %collective-permute-start.17 = (bf16[128,4096]{1,0:T(8,128)(2,1)S(1)}, bf16[128,4096]{1,0:T(8,128)(2,1)S(1)}, u32[]{:S(2)}, u32[]{:S(2)}) collective-permute-start(bf16[128,4096]{1,0:T(8,128)(2,1)S(1)} %get-tuple-element.40), channel_id=1, source_target_pairs={{0,2},{1,6},{2,10},{3,14},{4,3},{5,7},{6,11},{7,15},{8,0},{9,4},{1... | collective-permute-start | bytes 3145736 | tf_op jit(solution)/shard_map/dressed_1_2/ppermute | solution.py:77
  374.3 95.5 %collective-permute-start.21 = (bf16[256,4096]{1,0:T(8,128)(2,1)}, bf16[256,4096]{1,0:T(8,128)(2,1)S(1)}, u32[]{:S(2)}, u32[]{:S(2)}) collective-permute-start(bf16[256,4096]{1,0:T(8,128)(2,1)} %pad_maximum_fusion.5), channel_id=1, source_target_pairs={{0,4},{1,5},{2,6},{3,7},{4,0},{5,1},{6,2},{7,3},{8,12},{9,13},{10,... | collective-permute-start | bytes 6291464 | tf_op jit(solution)/shard_map/y_core_1/ppermute | solution.py:77
  402.8 62.7 %collective-permute-start.20 = (bf16[128,4096]{1,0:T(8,128)(2,1)S(1)}, bf16[128,4096]{1,0:T(8,128)(2,1)S(1)}, u32[]{:S(2)}, u32[]{:S(2)}) collective-permute-start(bf16[128,4096]{1,0:T(8,128)(2,1)S(1)} %get-tuple-element.40), channel_id=1, source_target_pairs={{0,3},{1,7},{2,11},{3,15},{4,2},{5,6},{6,10},{7,14},{8,1},{9,5},{1... | collective-permute-start | bytes 3145736 | tf_op jit(solution)/shard_map/dressed_1_3/ppermute | solution.py:77
  (12 other events, 96.1 us)

commit v2 on v1

--- a/solution.py
+++ b/solution.py
@@ -82,7 +82,8 @@
 
 
 def chunk_sizes(depth):
-    return [depth // 2] * 2
+    side = 5 * depth // 16
+    return [side, depth - 2 * side, side]
 
 
 def fetch(turn, dealt, dst, sem):
@@ -214,45 +215,61 @@
     n = len(sizes)
     own = [lax.slice_in_dim(cholesky, sum(sizes[:c]), sum(sizes[:c + 1]), axis=0) for c in range(n)]
 
-    previous = [()] * SIDE
-
-    def dealt(a, name, gate=()):
-        got = []
+    values = {}
+
+    def stage(names):
+        held = lax.optimization_barrier(tuple(values[k] for k in names))
+        values.update(zip(names, held))
+
+    def deal_out(key, source, c):
         for i in range(SIDE):
-            waits = previous[i] + (tuple(gate) if i == SIDE - 1 else ())
-            got.append(send(after(a, *waits), deal(i), "%s_%d" % (name, i)))
-        previous[:] = [(g,) for g in got]
-        return got
-
-    chol, sums, lean, other = [], [], [], []
-    rows, cols = [], []
-
-    def start_sums(c):
-        keep, give = dress(after(turn, *other[-1:]), chol[c], amplitudes)
-        both = keep + send(give, plane(1), "sum_core_%d" % c).astype(F32)
-        mine = both[:sizes[c]] + own[c].astype(F32)
-        sums.append((mine, both[sizes[c]:]))
-        lean.append(cat(*sums[c]).astype(BF16))
-        other.append(send(after(lean[c], *other[-1:]), plane(2), "sum_x_%d" % c))
-
+            values["%s%d_%d" % (key, c, i)] = send(values[source], deal(i), "%s_%d_%d" % (key, c, i))
+        return ["%s%d_%d" % (key, c, i) for i in range(SIDE)]
+
+    dealt = lambda key, c: [values["%s%d_%d" % (key, c, i)] for i in range(SIDE)]
+    cols, rows = {}, {}
     for c in range(n):
-        chol.append(dealt(own[c], "factors_%d" % c, lean[-1:] if c >= 2 else ()))
-        if c >= 1:
-            start_sums(c - 1)
-    start_sums(n - 1)
-
-    early = None
-    for c in range(n):
-        kq = sizes[c]
-        y0 = (sums[c][0] + other[c][kq:].astype(F32)).astype(BF16)
-        y2 = (sums[c][1] + other[c][:kq].astype(F32)).astype(BF16)
-        core = send(cat(y0, y2), plane(1), "y_core_%d" % c)
-        cols.append(cat(y0, core[:kq], y2, core[kq:]))
-        if c == n - 1:
-            early = gram(rows, cols[:c], gap_rows, gap_cols, None)
-        gate = (early,) if c == n - 1 else lean[-1:]
-        rows.append(pick(turn, dealt(y0, "dressed_%d" % c, gate)))
-    return gram(rows[n - 1:], cols[n - 1:], gap_rows, gap_cols, early)
+        values["own%d" % c] = own[c]
+    for t in range(2 * n):
+        names = []
+        if 2 <= t < n + 2:
+            c = t - 2
+            both = values["keep%d" % c] + send(values["give%d" % c], plane(1), "sum_core_%d" % c).astype(F32)
+            values["mine%d" % c] = both[:sizes[c]] + own[c].astype(F32)
+            values["second%d" % c] = both[sizes[c]:]
+            lean = cat(values["mine%d" % c], values["second%d" % c]).astype(BF16)
+            values["other%d" % c] = send(lean, plane(2), "sum_x_%d" % c)
+            names += ["mine%d" % c, "second%d" % c, "other%d" % c]
+        if t < n:
+            names += deal_out("factors", "own%d" % t, t)
+        if t >= n:
+            c = t - n
+            kq = sizes[c]
+            y0 = (values["mine%d" % c] + values["other%d" % c][kq:].astype(F32)).astype(BF16)
+            y2 = (values["second%d" % c] + values["other%d" % c][:kq].astype(F32)).astype(BF16)
+            values["y%d" % c] = y0
+            names += deal_out("dressed", "y%d" % c, c)
+            core = send(cat(y0, y2), plane(1), "y_core_%d" % c)
+            cols[c] = cat(y0, core[:kq], y2, core[kq:])
+        if 1 <= t <= n:
+            c = t - 1
+            values["keep%d" % c], values["give%d" % c] = dress(values["turn"], dealt("factors", c), amplitudes)
+            names += ["keep%d" % c, "give%d" % c]
+        if t > n:
+            c = t - n - 1
+            rows[c] = pick(turn, dealt("dressed", c))
+        if t == 2 * n - 1:
+            at = range(n - 1)
+            values["early"] = gram([rows[c] for c in at], [cols[c] for c in at], gap_rows, gap_cols, None)
+            names += ["early"]
+        for c in range(n):
+            if c > t and c < n:
+                names.append("own%d" % c)
+        values.setdefault("turn", turn)
+        stage(names + ["turn"])
+    last = n - 1
+    rows[last] = pick(turn, dealt("dressed", last))
+    return gram([rows[last]], [cols[last]], gap_rows, gap_cols, values["early"])
 
 
 def solution(mesh):

time: 508 us -> 500 us (0.984)
  starting transfers between devices: 75.3 us -> 43.9 us
  Pallas kernels: 113 us -> 138 us
  waiting for transfers between devices: 285 us -> 266 us
  local copies, waits for them, and re-layouts: 7.62 us -> 21.3 us
    ppermute x22 -> x33, starting transfers between devices: 75.3 us -> 43.9 us  [send(): return lax.ppermute(a, AXES, edges)]
    ppermute x22 -> x33, waiting for transfers between devices: 285 us -> 266 us  [send(): return lax.ppermute(a, AXES, edges)]
    pallas_call x2, Pallas kernels: 58 us -> 74.3 us  [gram(): pl.pallas_call(kernel, grid=(height // tile,), out_shape=jax.ShapeDtypeSt...]
    unnamed x28 -> x44, local copies, waits for them, and re-layouts: 1.77 us -> 13.7 us
    pallas_call x2 -> x3, Pallas kernels: 47.8 us -> 57.2 us  [dress(): pl.pallas_call(kernel, grid=(width // tile,), out_shape=[jax.ShapeDtypeSt...]
    another operation x1 -> x3, other arithmetic: 0.24 us -> 5.84 us
    concatenate x6 -> x9, other arithmetic: 11.7 us -> 7.92 us  [four(): cat = lambda *a: jnp.concatenate(a, axis=0)]
  transfers between devices with their start and end apart: 22 -> 33, of which waited for: 13 -> 19; matrix products, arithmetic and copies ran while one was open for 3% -> 5% of each run, Pallas kernels for 6% -> 21%
where the time goes in v2:
time: 500 us; the launch traced here: 497 us
  waiting for transfers between devices  266 us (53%)
  Pallas kernels  138 us (28%)
  starting transfers between devices  43.9 us (9%)
  other arithmetic  27.5 us (6%)
  local copies, waits for them, and re-layouts  21.3 us (4%)
    ppermute x33, waiting for transfers between devices, send(): return lax.ppermute(a, AXES, edges)  266 us
    pallas_call x2, Pallas kernels, gram(): pl.pallas_call(kernel, grid=(height // tile,), out_shape=jax.ShapeDtypeSt...  74.3 us
    pallas_call x3, Pallas kernels, dress(): pl.pallas_call(kernel, grid=(width // tile,), out_shape=[jax.ShapeDtypeSt...  57.2 us
    ppermute x33, starting transfers between devices, send(): return lax.ppermute(a, AXES, edges)  43.9 us
    unnamed x44, local copies, waits for them, and re-layouts  13.7 us
  transfers between devices with their start and end apart: 33, of which 19 were waited for; matrix products, arithmetic and copies ran while one was open for 5% of the time, Pallas kernels for 21%

profile of v2, /device:TPU:6, one launch (start us, length us, event | category | flops | bytes accessed | tf_op | source)
XLA Modules:
  0.0 497.4 jit_solution(11053577575174131677)
XLA Ops:
  7.3 3.6 collective-permute-start
  12.9 34.9 %collective-permute-done.3.rest_3_ = bf16[80,4096]{1,0:T(8,128)(2,1)S(1)} collective-permute-done((bf16[80,4096]{1,0:T(8,128)(2,1)S(1)}, bf16[80,4096]{1,0:T(8,128)(2,1)S(1)}, u32[]{:S(2)}, u32[]{:S(2)}) %collective-permute-start.3) | collective-permute-done | bytes 655392 | tf_op jit(solution)/shard_map/factors_0_3/ppermute | solution.py:77
  47.8 48.2 %collective-permute-done.2.rest_2_ = bf16[80,4096]{1,0:T(8,128)(2,1)S(1)} collective-permute-done((bf16[80,4096]{1,0:T(8,128)(2,1)S(1)}, bf16[80,4096]{1,0:T(8,128)(2,1)S(1)}, u32[]{:S(2)}, u32[]{:S(2)}) %collective-permute-start.2) | collective-permute-done | bytes 655392 | tf_op jit(solution)/shard_map/factors_0_2/ppermute | solution.py:77
  98.6 5.0 %collective-permute-start.5 = (bf16[96,4096]{1,0:T(8,128)(2,1)}, bf16[96,4096]{1,0:T(8,128)(2,1)S(1)}, u32[]{:S(2)}, u32[]{:S(2)}) collective-permute-start(bf16[96,4096]{1,0:T(8,128)(2,1)} %slice.64), channel_id=1, source_target_pairs={{0,1},{1,5},{2,9},{3,13},{4,0},{5,4},{6,8},{7,12},{8,3},{9,7},{10,... | collective-permute-start | bytes 2359304 | tf_op jit(solution)/shard_map/factors_1_1/ppermute | solution.py:77
  108.8 18.7 %dress.3 = (f32[160,4096]{1,0:T(8,128)}, bf16[160,4096]{1,0:T(8,128)(2,1)S(1)}) custom-call(s32[1]{0:T(128)} %bitcast.turn_ref, bf16[4096,4096]{1,0:T(8,128)(2,1)} %t_ref.5, bf16[80,4096]{1,0:T(8,128)(2,1)S(1)} %copy-done.15, bf16[80,4096]{1,0:T(8,128)(2,1)S(1)} %copy-done.13, bf16[80,4096]{1,0:T(8,128)(2,1)S(1)} %copy-done.11, ...), custom_call_target="tpu_custom_call" | custom-call | flops 10737418240 | bytes 40108032 | tf_op jit(solution)/shard_map/dress/pallas_call | solution.py:140
  127.5 7.3 %collective-permute-done.6.rest_2_ = bf16[96,4096]{1,0:T(8,128)(2,1)S(1)} collective-permute-done((bf16[96,4096]{1,0:T(8,128)(2,1)}, bf16[96,4096]{1,0:T(8,128)(2,1)S(1)}, u32[]{:S(2)}, u32[]{:S(2)}) %collective-permute-start.6) | collective-permute-done | bytes 786464 | tf_op jit(solution)/shard_map/factors_1_2/ppermute | solution.py:77
  134.9 19.3 %collective-permute-done.5.rest_1_ = bf16[96,4096]{1,0:T(8,128)(2,1)S(1)} collective-permute-done((bf16[96,4096]{1,0:T(8,128)(2,1)}, bf16[96,4096]{1,0:T(8,128)(2,1)S(1)}, u32[]{:S(2)}, u32[]{:S(2)}) %collective-permute-start.5) | collective-permute-done | bytes 786464 | tf_op jit(solution)/shard_map/factors_1_1/ppermute | solution.py:77
  155.0 15.6 %collective-permute-done.4.rest_0_ = bf16[96,4096]{1,0:T(8,128)(2,1)S(1)} collective-permute-done((bf16[96,4096]{1,0:T(8,128)(2,1)}, bf16[96,4096]{1,0:T(8,128)(2,1)S(1)}, u32[]{:S(2)}, u32[]{:S(2)}) %collective-permute-start.4) | collective-permute-done | bytes 786464 | tf_op jit(solution)/shard_map/factors_1_0/ppermute | solution.py:77
  185.7 3.3 collective-permute-start.11
  190.9 19.8 %dress.4 = (f32[192,4096]{1,0:T(8,128)}, bf16[192,4096]{1,0:T(8,128)(2,1)}) custom-call(s32[1]{0:T(128)} %bitcast.turn_ref, bf16[4096,4096]{1,0:T(8,128)(2,1)} %t_ref.5, bf16[96,4096]{1,0:T(8,128)(2,1)S(1)} %copy-done.3, bf16[96,4096]{1,0:T(8,128)(2,1)S(1)} %copy-done.1, bf16[96,4096]{1,0:T(8,128)(2,1)S(1)} %collective-permute-done.6.rest_2_, ...), custom_call_target="tpu_custom_call" | custom-call | flops 12884901888 | bytes 41418752 | tf_op jit(solution)/shard_map/dress/pallas_call | solution.py:140
  210.7 19.3 %collective-permute-done.13.rest_3_ = bf16[80,4096]{1,0:T(8,128)(2,1)S(1)} collective-permute-done((bf16[80,4096]{1,0:T(8,128)(2,1)S(1)}, bf16[80,4096]{1,0:T(8,128)(2,1)S(1)}, u32[]{:S(2)}, u32[]{:S(2)}) %collective-permute-start.13) | collective-permute-done | bytes 655392 | tf_op jit(solution)/shard_map/factors_2_3/ppermute | solution.py:77
  230.0 13.8 %collective-permute-done.12.rest_2_ = bf16[80,4096]{1,0:T(8,128)(2,1)S(1)} collective-permute-done((bf16[80,4096]{1,0:T(8,128)(2,1)S(1)}, bf16[80,4096]{1,0:T(8,128)(2,1)S(1)}, u32[]{:S(2)}, u32[]{:S(2)}) %collective-permute-start.12) | collective-permute-done | bytes 655392 | tf_op jit(solution)/shard_map/factors_2_2/ppermute | solution.py:77
  252.9 3.9 collective-permute-start.17
  263.3 18.7 %dress.5 = (f32[160,4096]{1,0:T(8,128)}, bf16[160,4096]{1,0:T(8,128)(2,1)S(1)}) custom-call(s32[1]{0:T(128)} %bitcast.turn_ref, bf16[4096,4096]{1,0:T(8,128)(2,1)} %t_ref.5, bf16[80,4096]{1,0:T(8,128)(2,1)S(1)} %copy-done.9, bf16[80,4096]{1,0:T(8,128)(2,1)S(1)} %copy-done.7, bf16[80,4096]{1,0:T(8,128)(2,1)S(1)} %copy-done.5, ...), custom_call_target="tpu_custom_call" | custom-call | flops 10737418240 | bytes 40108032 | tf_op jit(solution)/shard_map/dress/pallas_call | solution.py:140
  287.1 10.7 %collective-permute-done.19.rest_3_ = bf16[80,4096]{1,0:T(8,128)(2,1)S(1)} collective-permute-done((bf16[80,4096]{1,0:T(8,128)(2,1)S(1)}, bf16[80,4096]{1,0:T(8,128)(2,1)S(1)}, u32[]{:S(2)}, u32[]{:S(2)}) %collective-permute-start.19) | collective-permute-done | bytes 655392 | tf_op jit(solution)/shard_map/dressed_0_3/ppermute | solution.py:77
  297.8 13.6 %collective-permute-done.18.rest_2_ = bf16[80,4096]{1,0:T(8,128)(2,1)S(1)} collective-permute-done((bf16[80,4096]{1,0:T(8,128)(2,1)S(1)}, bf16[80,4096]{1,0:T(8,128)(2,1)S(1)}, u32[]{:S(2)}, u32[]{:S(2)}) %collective-permute-start.18) | collective-permute-done | bytes 655392 | tf_op jit(solution)/shard_map/dressed_0_2/ppermute | solution.py:77
  311.4 3.7 collective-permute-done.16.rest_0_
  315.1 7.9 %collective-permute-done.15 = bf16[192,4096]{1,0:T(8,128)(2,1)} collective-permute-done((bf16[192,4096]{1,0:T(8,128)(2,1)}, bf16[192,4096]{1,0:T(8,128)(2,1)}, u32[]{:S(2)}, u32[]{:S(2)}) %collective-permute-start.15) | collective-permute-done | bytes 1572896 | tf_op jit(solution)/shard_map/sum_x_1/ppermute | solution.py:77
  341.3 37.6 %collective-permute-done.25.rest_3_ = bf16[96,4096]{1,0:T(8,128)(2,1)S(1)} collective-permute-done((bf16[96,4096]{1,0:T(8,128)(2,1)S(1)}, bf16[96,4096]{1,0:T(8,128)(2,1)S(1)}, u32[]{:S(2)}, u32[]{:S(2)}) %collective-permute-start.25) | collective-permute-done | bytes 786464 | tf_op jit(solution)/shard_map/dressed_1_3/ppermute | solution.py:77
  379.0 17.1 %collective-permute-done.24.rest_2_ = bf16[96,4096]{1,0:T(8,128)(2,1)S(1)} collective-permute-done((bf16[96,4096]{1,0:T(8,128)(2,1)S(1)}, bf16[96,4096]{1,0:T(8,128)(2,1)S(1)}, u32[]{:S(2)}, u32[]{:S(2)}) %collective-permute-start.24) | collective-permute-done | bytes 786464 | tf_op jit(solution)/shard_map/dressed_1_2/ppermute | solution.py:77
  399.7 3.2 collective-permute-start.28
  408.8 41.6 %gram.2.refs_4_ = bf16[4096,4096]{1,0:T(8,128)(2,1)} custom-call(bf16[320,4096]{1,0:T(8,128)(2,1)} %pick.3.refs_0_, bf16[384,4096]{1,0:T(8,128)(2,1)} %pick.4.refs_1_, bf16[320,4096]{1,0:T(8,128)(2,1)} %pad_maximum_fusion.1.refs_2_, bf16[384,4096]{1,0:T(8,128)(2,1)} %pad_maximum_fusion.refs_3_, f32[4096,1]{1,0:T(8,128)S(1)} %copy.10.refs_4_.refs_2_, ...), custom_call_target="tpu_custom_call" | custom-call | flops 23622320128 | bytes 33554432 | tf_op jit(solution)/shard_map/gram/pallas_call | solution.py:190
  450.4 8.5 %collective-permute-done.28.rest_2_ = bf16[80,4096]{1,0:T(8,128)(2,1)S(1)} collective-permute-done((bf16[80,4096]{1,0:T(8,128)(2,1)S(1)}, bf16[80,4096]{1,0:T(8,128)(2,1)S(1)}, u32[]{:S(2)}, u32[]{:S(2)}) %collective-permute-start.28) | collective-permute-done | bytes 655392 | tf_op jit(solution)/shard_map/dressed_2_2/ppermute | solution.py:77
  464.7 32.8 %gram.3 = bf16[4096,4096]{1,0:T(8,128)(2,1)} custom-call(bf16[320,4096]{1,0:T(8,128)(2,1)} %pick.5.refs_0_, bf16[320,4096]{1,0:T(8,128)(2,1)} %pad_maximum_fusion.2.refs_1_, f32[4096,1]{1,0:T(8,128)S(1)} %copy.10.refs_4_.refs_2_, f32[1,4096]{1,0:T(1,128)S(1)} %bitcast.4, bf16[4096,4096]{1,0:T(8,128)(2,1)} %gram.2.refs_4_), custom_call_target="tpu_custom_call", output_to_operand_aliasing={{}: (4, {})} | custom-call | flops 10737418240 | bytes 67108864 | tf_op jit(solution)/shard_map/gram/pallas_call | solution.py:190
  (126 shorter events, 88.9 us)
Async XLA Ops:
  3.8 92.2 %collective-permute-start.2 = (bf16[80,4096]{1,0:T(8,128)(2,1)S(1)}, bf16[80,4096]{1,0:T(8,128)(2,1)S(1)}, u32[]{:S(2)}, u32[]{:S(2)}) collective-permute-start(bf16[80,4096]{1,0:T(8,128)(2,1)S(1)} %get-tuple-element.123), channel_id=1, source_target_pairs={{0,2},{1,6},{2,10},{3,14},{4,3},{5,7},{6,11},{7,15},{8,0},{9,4},{1... | collective-permute-start | bytes 1966088 | tf_op jit(solution)/shard_map/factors_0_2/ppermute | solution.py:77
  6.4 90.5 %collective-permute-start.1 = (bf16[80,4096]{1,0:T(8,128)(2,1)S(1)}, bf16[80,4096]{1,0:T(8,128)(2,1)S(1)}, u32[]{:S(2)}, u32[]{:S(2)}) collective-permute-start(bf16[80,4096]{1,0:T(8,128)(2,1)S(1)} %get-tuple-element.123), channel_id=1, source_target_pairs={{0,1},{1,5},{2,9},{3,13},{4,0},{5,4},{6,8},{7,12},{8,3},{9,7},{10,... | collective-permute-start | bytes 1966088 | tf_op jit(solution)/shard_map/factors_0_1/ppermute | solution.py:77
  7.3 90.5 %collective-permute-start = (bf16[80,4096]{1,0:T(8,128)(2,1)S(1)}, bf16[80,4096]{1,0:T(8,128)(2,1)S(1)}, u32[]{:S(2)}, u32[]{:S(2)}) collective-permute-start(bf16[80,4096]{1,0:T(8,128)(2,1)S(1)} %get-tuple-element.123), channel_id=1, source_target_pairs={{0,0},{1,4},{2,8},{3,12},{4,1},{5,5},{6,9},{7,13},{8,2},{9,6},{10,... | collective-permute-start | bytes 1966088 | tf_op jit(solution)/shard_map/factors_0_0/ppermute | solution.py:77
  98.6 55.6 %collective-permute-start.5 = (bf16[96,4096]{1,0:T(8,128)(2,1)}, bf16[96,4096]{1,0:T(8,128)(2,1)S(1)}, u32[]{:S(2)}, u32[]{:S(2)}) collective-permute-start(bf16[96,4096]{1,0:T(8,128)(2,1)} %slice.64), channel_id=1, source_target_pairs={{0,1},{1,5},{2,9},{3,13},{4,0},{5,4},{6,8},{7,12},{8,3},{9,7},{10,... | collective-permute-start | bytes 2359304 | tf_op jit(solution)/shard_map/factors_1_1/ppermute | solution.py:77
  103.6 67.0 %collective-permute-start.4 = (bf16[96,4096]{1,0:T(8,128)(2,1)}, bf16[96,4096]{1,0:T(8,128)(2,1)S(1)}, u32[]{:S(2)}, u32[]{:S(2)}) collective-permute-start(bf16[96,4096]{1,0:T(8,128)(2,1)} %slice.64), channel_id=1, source_target_pairs={{0,0},{1,4},{2,8},{3,12},{4,1},{5,5},{6,9},{7,13},{8,2},{9,6},{10,... | collective-permute-start | bytes 2359304 | tf_op jit(solution)/shard_map/factors_1_0/ppermute | solution.py:77
  180.3 67.2 %collective-permute-start.9 = (bf16[160,4096]{1,0:T(8,128)(2,1)S(1)}, bf16[160,4096]{1,0:T(8,128)(2,1)S(1)}, u32[]{:S(2)}, u32[]{:S(2)}) collective-permute-start(bf16[160,4096]{1,0:T(8,128)(2,1)S(1)} %pad_maximum_fusion.5), channel_id=1, source_target_pairs={{0,8},{1,9},{2,10},{3,11},{4,12},{5,13},{6,14},{7,15},{8,0},{9,1},... | collective-permute-start | bytes 3932168 | tf_op jit(solution)/shard_map/sum_x_0/ppermute | solution.py:77
  183.9 46.1 %collective-permute-start.13 = (bf16[80,4096]{1,0:T(8,128)(2,1)S(1)}, bf16[80,4096]{1,0:T(8,128)(2,1)S(1)}, u32[]{:S(2)}, u32[]{:S(2)}) collective-permute-start(bf16[80,4096]{1,0:T(8,128)(2,1)S(1)} %copy-done.19), channel_id=1, source_target_pairs={{0,3},{1,7},{2,11},{3,15},{4,2},{5,6},{6,10},{7,14},{8,1},{9,5},{1... | collective-permute-start | bytes 1966088 | tf_op jit(solution)/shard_map/factors_2_3/ppermute | solution.py:77
  185.7 58.0 %collective-permute-start.12 = (bf16[80,4096]{1,0:T(8,128)(2,1)S(1)}, bf16[80,4096]{1,0:T(8,128)(2,1)S(1)}, u32[]{:S(2)}, u32[]{:S(2)}) collective-permute-start(bf16[80,4096]{1,0:T(8,128)(2,1)S(1)} %copy-done.19), channel_id=1, source_target_pairs={{0,2},{1,6},{2,10},{3,14},{4,3},{5,7},{6,11},{7,15},{8,0},{9,4},{1... | collective-permute-start | bytes 1966088 | tf_op jit(solution)/shard_map/factors_2_2/ppermute | solution.py:77
  185.7 58.9 %collective-permute-start.11 = (bf16[80,4096]{1,0:T(8,128)(2,1)S(1)}, bf16[80,4096]{1,0:T(8,128)(2,1)S(1)}, u32[]{:S(2)}, u32[]{:S(2)}) collective-permute-start(bf16[80,4096]{1,0:T(8,128)(2,1)S(1)} %copy-done.19), channel_id=1, source_target_pairs={{0,1},{1,5},{2,9},{3,13},{4,0},{5,4},{6,8},{7,12},{8,3},{9,7},{10,... | collective-permute-start | bytes 1966088 | tf_op jit(solution)/shard_map/factors_2_1/ppermute | solution.py:77
  189.0 57.5 %collective-permute-start.10 = (bf16[80,4096]{1,0:T(8,128)(2,1)S(1)}, bf16[80,4096]{1,0:T(8,128)(2,1)S(1)}, u32[]{:S(2)}, u32[]{:S(2)}) collective-permute-start(bf16[80,4096]{1,0:T(8,128)(2,1)S(1)} %copy-done.19), channel_id=1, source_target_pairs={{0,0},{1,4},{2,8},{3,12},{4,1},{5,5},{6,9},{7,13},{8,2},{9,6},{10,... | collective-permute-start | bytes 1966088 | tf_op jit(solution)/shard_map/factors_2_0/ppermute | solution.py:77
  251.7 46.1 %collective-permute-start.19 = (bf16[80,4096]{1,0:T(8,128)(2,1)S(1)}, bf16[80,4096]{1,0:T(8,128)(2,1)S(1)}, u32[]{:S(2)}, u32[]{:S(2)}) collective-permute-start(bf16[80,4096]{1,0:T(8,128)(2,1)S(1)} %get-tuple-element.135), channel_id=1, source_target_pairs={{0,3},{1,7},{2,11},{3,15},{4,2},{5,6},{6,10},{7,14},{8,1},{9,5},{1... | collective-permute-start | bytes 1966088 | tf_op jit(solution)/shard_map/dressed_0_3/ppermute | solution.py:77
  251.8 59.6 %collective-permute-start.18 = (bf16[80,4096]{1,0:T(8,128)(2,1)S(1)}, bf16[80,4096]{1,0:T(8,128)(2,1)S(1)}, u32[]{:S(2)}, u32[]{:S(2)}) collective-permute-start(bf16[80,4096]{1,0:T(8,128)(2,1)S(1)} %get-tuple-element.135), channel_id=1, source_target_pairs={{0,2},{1,6},{2,10},{3,14},{4,3},{5,7},{6,11},{7,15},{8,0},{9,4},{1... | collective-permute-start | bytes 1966088 | tf_op jit(solution)/shard_map/dressed_0_2/ppermute | solution.py:77
  252.9 58.4 %collective-permute-start.17 = (bf16[80,4096]{1,0:T(8,128)(2,1)S(1)}, bf16[80,4096]{1,0:T(8,128)(2,1)S(1)}, u32[]{:S(2)}, u32[]{:S(2)}) collective-permute-start(bf16[80,4096]{1,0:T(8,128)(2,1)S(1)} %get-tuple-element.135), channel_id=1, source_target_pairs={{0,1},{1,5},{2,9},{3,13},{4,0},{5,4},{6,8},{7,12},{8,3},{9,7},{10,... | collective-permute-start | bytes 1966088 | tf_op jit(solution)/shard_map/dressed_0_1/ppermute | solution.py:77
  262.5 60.5 %collective-permute-start.15 = (bf16[192,4096]{1,0:T(8,128)(2,1)}, bf16[192,4096]{1,0:T(8,128)(2,1)}, u32[]{:S(2)}, u32[]{:S(2)}) collective-permute-start(bf16[192,4096]{1,0:T(8,128)(2,1)} %pad_maximum_fusion.3), channel_id=1, source_target_pairs={{0,8},{1,9},{2,10},{3,11},{4,12},{5,13},{6,14},{7,15},{8,0},{9,1},... | collective-permute-start | bytes 4718600 | tf_op jit(solution)/shard_map/sum_x_1/ppermute | solution.py:77
  324.8 54.2 %collective-permute-start.25 = (bf16[96,4096]{1,0:T(8,128)(2,1)S(1)}, bf16[96,4096]{1,0:T(8,128)(2,1)S(1)}, u32[]{:S(2)}, u32[]{:S(2)}) collective-permute-start(bf16[96,4096]{1,0:T(8,128)(2,1)S(1)} %get-tuple-element.127), channel_id=1, source_target_pairs={{0,3},{1,7},{2,11},{3,15},{4,2},{5,6},{6,10},{7,14},{8,1},{9,5},{1... | collective-permute-start | bytes 2359304 | tf_op jit(solution)/shard_map/dressed_1_3/ppermute | solution.py:77
  325.0 71.1 %collective-permute-start.24 = (bf16[96,4096]{1,0:T(8,128)(2,1)S(1)}, bf16[96,4096]{1,0:T(8,128)(2,1)S(1)}, u32[]{:S(2)}, u32[]{:S(2)}) collective-permute-start(bf16[96,4096]{1,0:T(8,128)(2,1)S(1)} %get-tuple-element.127), channel_id=1, source_target_pairs={{0,2},{1,6},{2,10},{3,14},{4,3},{5,7},{6,11},{7,15},{8,0},{9,4},{1... | collective-permute-start | bytes 2359304 | tf_op jit(solution)/shard_map/dressed_1_2/ppermute | solution.py:77
  328.1 68.0 %collective-permute-start.23 = (bf16[96,4096]{1,0:T(8,128)(2,1)S(1)}, bf16[96,4096]{1,0:T(8,128)(2,1)S(1)}, u32[]{:S(2)}, u32[]{:S(2)}) collective-permute-start(bf16[96,4096]{1,0:T(8,128)(2,1)S(1)} %get-tuple-element.127), channel_id=1, source_target_pairs={{0,1},{1,5},{2,9},{3,13},{4,0},{5,4},{6,8},{7,12},{8,3},{9,7},{10,... | collective-permute-start | bytes 2359304 | tf_op jit(solution)/shard_map/dressed_1_1/ppermute | solution.py:77
  329.8 67.1 %collective-permute-start.22 = (bf16[96,4096]{1,0:T(8,128)(2,1)S(1)}, bf16[96,4096]{1,0:T(8,128)(2,1)S(1)}, u32[]{:S(2)}, u32[]{:S(2)}) collective-permute-start(bf16[96,4096]{1,0:T(8,128)(2,1)S(1)} %get-tuple-element.127), channel_id=1, source_target_pairs={{0,0},{1,4},{2,8},{3,12},{4,1},{5,5},{6,9},{7,13},{8,2},{9,6},{10,... | collective-permute-start | bytes 2359304 | tf_op jit(solution)/shard_map/dressed_1_0/ppermute | solution.py:77
  339.3 60.0 %collective-permute-start.21 = (bf16[160,4096]{1,0:T(8,128)(2,1)S(1)}, bf16[160,4096]{1,0:T(8,128)(2,1)S(1)}, u32[]{:S(2)}, u32[]{:S(2)}) collective-permute-start(bf16[160,4096]{1,0:T(8,128)(2,1)S(1)} %pad_maximum_fusion.6), channel_id=1, source_target_pairs={{0,8},{1,9},{2,10},{3,11},{4,12},{5,13},{6,14},{7,15},{8,0},{9,1},... | collective-permute-start | bytes 3932168 | tf_op jit(solution)/shard_map/sum_x_2/ppermute | solution.py:77
  399.6 50.8 %collective-permute-start.29 = (bf16[80,4096]{1,0:T(8,128)(2,1)S(1)}, bf16[80,4096]{1,0:T(8,128)(2,1)S(1)}, u32[]{:S(2)}, u32[]{:S(2)}) collective-permute-start(bf16[80,4096]{1,0:T(8,128)(2,1)S(1)} %get-tuple-element.131), channel_id=1, source_target_pairs={{0,3},{1,7},{2,11},{3,15},{4,2},{5,6},{6,10},{7,14},{8,1},{9,5},{1... | collective-permute-start | bytes 1966088 | tf_op jit(solution)/shard_map/dressed_2_3/ppermute | solution.py:77
  399.7 59.2 %collective-permute-start.28 = (bf16[80,4096]{1,0:T(8,128)(2,1)S(1)}, bf16[80,4096]{1,0:T(8,128)(2,1)S(1)}, u32[]{:S(2)}, u32[]{:S(2)}) collective-permute-start(bf16[80,4096]{1,0:T(8,128)(2,1)S(1)} %get-tuple-element.131), channel_id=1, source_target_pairs={{0,2},{1,6},{2,10},{3,14},{4,3},{5,7},{6,11},{7,15},{8,0},{9,4},{1... | collective-permute-start | bytes 1966088 | tf_op jit(solution)/shard_map/dressed_2_2/ppermute | solution.py:77
  403.0 55.9 %collective-permute-start.27 = (bf16[80,4096]{1,0:T(8,128)(2,1)S(1)}, bf16[80,4096]{1,0:T(8,128)(2,1)S(1)}, u32[]{:S(2)}, u32[]{:S(2)}) collective-permute-start(bf16[80,4096]{1,0:T(8,128)(2,1)S(1)} %get-tuple-element.131), channel_id=1, source_target_pairs={{0,1},{1,5},{2,9},{3,13},{4,0},{5,4},{6,8},{7,12},{8,3},{9,7},{10,... | collective-permute-start | bytes 1966088 | tf_op jit(solution)/shard_map/dressed_2_1/ppermute | solution.py:77
  404.7 55.9 %collective-permute-start.26 = (bf16[80,4096]{1,0:T(8,128)(2,1)S(1)}, bf16[80,4096]{1,0:T(8,128)(2,1)S(1)}, u32[]{:S(2)}, u32[]{:S(2)}) collective-permute-start(bf16[80,4096]{1,0:T(8,128)(2,1)S(1)} %get-tuple-element.131), channel_id=1, source_target_pairs={{0,0},{1,4},{2,8},{3,12},{4,1},{5,5},{6,9},{7,13},{8,2},{9,6},{10,... | collective-permute-start | bytes 1966088 | tf_op jit(solution)/shard_map/dressed_2_0/ppermute | solution.py:77
  406.8 56.2 %collective-permute-start.32 = (bf16[160,4096]{1,0:T(8,128)(2,1)S(1)}, bf16[160,4096]{1,0:T(8,128)(2,1)S(1)}, u32[]{:S(2)}, u32[]{:S(2)}) collective-permute-start(bf16[160,4096]{1,0:T(8,128)(2,1)S(1)} %pad_maximum_fusion.8), channel_id=1, source_target_pairs={{0,4},{1,5},{2,6},{3,7},{4,0},{5,1},{6,2},{7,3},{8,12},{9,13},{10,... | collective-permute-start | bytes 3932168 | tf_op jit(solution)/shard_map/y_core_2/ppermute | solution.py:77
  (31 other events, 314.5 us)
